TPU v7x, 32 devices: a whole 2x2x4 slice. The times are simulated.
32 devices in a mesh: dp: 4 (over y, x), row: 2 (over core), col: 4 (over z).
Axes of the slice: x: 2, y: 2, z: 4, core: 2. Of those that a mesh axis runs over, the one named last changes fastest.
Arguments:
- step_count: int32 [1], replicated, may hold values from 2 to 11
- ffn_weight: bfloat16 [4096, 10240], P('row', 'col'), may hold values from -40 to 40
- ffn_grads: float32 [4, 4096, 10240], P('dp', 'row', 'col'), may hold values from -80 to 80
- ffn_rows: float32 [4096], P('row'), may hold values from 0.1 to 12
- ffn_cols: float32 [10240], P('col'), may hold values from 0.1 to 1
- attn_weight: bfloat16 [4096, 4096], P('row', 'col'), may hold values from -40 to 40
- attn_grads: float32 [4, 4096, 4096], P('dp', 'row', 'col'), may hold values from -80 to 80
- attn_rows: float32 [4096], P('row'), may hold values from 0.1 to 12
- attn_cols: float32 [4096], P('col'), may hold values from 0.1 to 1
Outputs:
- ffn_weight_new: float32 [4096, 10240], P('row', 'col')
- ffn_update: float32 [4096, 10240], P('row', 'col')
- ffn_rows_new: float32 [4096], P('row')
- ffn_cols_new: float32 [10240], P('col')
- attn_weight_new: float32 [4096, 4096], P('row', 'col')
- attn_update: float32 [4096, 4096], P('row', 'col')
- attn_rows_new: float32 [4096], P('row')
- attn_cols_new: float32 [4096], P('col')
All inputs are finite; a program needn't handle non-finite values.
Results may differ from a plain program's by a relative error of at most 0.0003.
Values sent between devices are 32-bit elements; how exact they have to be, the bound alone decides.
A program may use at most 320 MiB of HBM per device.

v0:
```python
import jax
import jax.numpy as jnp
from jax import lax
from jax.sharding import PartitionSpec as P


def apply_step(w_tile, factor, update):
    return w_tile.astype(jnp.float32) - factor * update


def body(
    step_count,
    ffn_weight,
    ffn_grads,
    ffn_rows,
    ffn_cols,
    attn_weight,
    attn_grads,
    attn_rows,
    attn_cols,
):
    step_value = step_count[0].astype(jnp.float32)
    decay = 1.0 - step_value ** (-0.8)
    weights = (ffn_weight, attn_weight)
    rows_old = (ffn_rows, attn_rows)
    cols_old = (ffn_cols, attn_cols)
    row_devs = lax.axis_size("row")
    col_devs = lax.axis_size("col")
    widths_in = tuple((w_tile.shape[0] * row_devs for w_tile in weights))
    widths_out = tuple((w_tile.shape[1] * col_devs for w_tile in weights))
    summed = (
        lax.psum_scatter(ffn_grads[0], "dp", scatter_dimension=0, tiled=True),
        lax.psum_scatter(attn_grads[0], "dp", scatter_dimension=0, tiled=True),
    )
    share_rows = summed[0].shape[0]
    offset = lax.axis_index("dp") * share_rows
    owned_tiles = tuple(
        (lax.dynamic_slice_in_dim(w_tile, offset, share_rows, 0) for w_tile in weights)
    )
    squares = tuple((g_part * g_part + 1e-30 for g_part in summed))
    row_sums = lax.psum(tuple((jnp.sum(s_part, axis=1) for s_part in squares)), "col")
    col_part = tuple((jnp.sum(s_part, axis=0) for s_part in squares))
    row_full = lax.all_gather(row_sums, "dp", axis=0, tiled=True)
    col_sums = lax.psum(col_part, ("dp", "row"))
    rows_new = tuple(
        (
            decay * rows_old[index] + (1.0 - decay) * (row_full[index] / widths_out[index])
            for index in range(2)
        )
    )
    cols_new = tuple(
        (
            decay * cols_old[index] + (1.0 - decay) * (col_sums[index] / widths_in[index])
            for index in range(2)
        )
    )
    masses = lax.psum(tuple((jnp.sum(r_tile) for r_tile in rows_new)), "row")
    raw_updates = []
    update_sq = []
    for index in range(2):
        row_own = lax.dynamic_slice_in_dim(rows_new[index], offset, share_rows, 0)
        second = row_own[:, None] * cols_new[index][None, :] / (masses[index] / widths_in[index])
        raw_update = summed[index] / jnp.sqrt(second)
        raw_updates.append(raw_update)
        update_sq.append(jnp.sum(raw_update * raw_update))
    update_tot = lax.psum((update_sq[0], update_sq[1]), ("dp", "row", "col"))
    weight_tot = lax.psum(
        tuple((jnp.sum(jnp.square(w_tile.astype(jnp.float32))) for w_tile in weights)),
        ("row", "col"),
    )
    totals = tuple(update_tot) + tuple(weight_tot)
    clipped = []
    factors = []
    for index in range(2):
        entries = widths_in[index] * widths_out[index]
        update_rms = jnp.sqrt(totals[index] / entries)
        clipped.append(raw_updates[index] / jnp.maximum(1.0, update_rms))
        factors.append(0.01 * jnp.sqrt(totals[2 + index] / entries))
    quarter_new = [
        apply_step(owned_tiles[index], factors[index], clipped[index]) for index in range(2)
    ]
    fresh = (
        lax.all_gather(quarter_new[0], "dp", axis=0, tiled=True),
        lax.all_gather(quarter_new[1], "dp", axis=0, tiled=True),
    )
    clipped = (
        lax.all_gather(clipped[0], "dp", axis=0, tiled=True),
        lax.all_gather(clipped[1], "dp", axis=0, tiled=True),
    )
    return (
        fresh[0],
        clipped[0],
        rows_new[0],
        cols_new[0],
        fresh[1],
        clipped[1],
        rows_new[1],
        cols_new[1],
    )


def solution(mesh):
    in_specs = (
        P(),
        P("row", "col"),
        P("dp", "row", "col"),
        P("row"),
        P("col"),
        P("row", "col"),
        P("dp", "row", "col"),
        P("row"),
        P("col"),
    )
    out_specs = (
        P("row", "col"),
        P("row", "col"),
        P("row"),
        P("col"),
        P("row", "col"),
        P("row", "col"),
        P("row"),
        P("col"),
    )
    return jax.shard_map(body, mesh=mesh, in_specs=in_specs, out_specs=out_specs, check_vma=False)
```

profile of v0, /device:TPU:0, one launch (start us, length us, event | category | flops | bytes accessed | tf_op | source)
XLA Modules:
  0.0 1013.2 jit_solution(17527655425020090493)
XLA Ops:
  7.2 0.7 reduce-scatter.5.cloned.1.call-update
  7.9 0.7 reduce-scatter.3.cloned.1.call-update
  8.7 10.1 multiply_reduce_fusion
  18.9 2.8 multiply_reduce_fusion.1
  21.6 19.1 %all-reduce.1 = (f32[]{:T(128)}, f32[]{:T(128)}) all-reduce(f32[]{:T(128)} %multiply_reduce_fusion, f32[]{:T(128)} %multiply_reduce_fusion.1), channel_id=1, replica_groups=mesh['dp'=4,'row'=2,'col'=4] {'row','col'}, use_global_device_ids=true, to_apply=%region_1.0 | all-reduce | flops 2 | bytes 16 | tf_op jit(solution)/shard_map/psum | solution.py:67
  42.2 58.1 %reduce-scatter.5.cloned.1.call-done = f32[512,1024]{1,0:T(8,128)} async-done(((f32[2048,1024]{1,0:T(8,128)}), f32[512,1024]{1,0:T(8,128)}) %reduce-scatter.5.cloned.1.call-update) | async-done | bytes 2097168 | tf_op jit(solution)/shard_map/reduce_scatter | solution.py:33
  100.2 2.1 fusion.2
  102.4 189.1 %reduce-scatter.3.cloned.1.call-done = f32[512,2560]{1,0:T(8,128)} async-done(((f32[2048,2560]{1,0:T(8,128)}), f32[512,2560]{1,0:T(8,128)}) %reduce-scatter.3.cloned.1.call-update) | async-done | bytes 5242896 | tf_op jit(solution)/shard_map/reduce_scatter | solution.py:32
  291.4 3.4 fusion
  294.9 11.7 %all-reduce.3 = (f32[512]{0:T(512)S(1)}, f32[512]{0:T(512)S(1)}) all-reduce(f32[512]{0:T(512)S(1)} %get-tuple-element.9, f32[512]{0:T(512)S(1)} %get-tuple-element.11), channel_id=1, replica_groups=mesh['dp'=4,'row'=2,'col'=4] {'col'}, use_global_device_ids=true, to_apply=%region_4.0 | all-reduce | flops 1024 | bytes 8192 | tf_op jit(solution)/shard_map/psum | solution.py:41
  306.5 7.9 all-gather.1
  314.5 7.2 all-gather
  321.7 0.6 fusion.4
  322.3 3.1 all-reduce.4
  326.7 0.1 dynamic_slice.15
  326.9 23.4 %all-reduce.2 = (f32[2560]{0:T(1024)S(1)}, f32[1024]{0:T(1024)S(1)}) all-reduce(f32[2560]{0:T(1024)S(1)} %get-tuple-element.8, f32[1024]{0:T(1024)S(1)} %get-tuple-element.10), channel_id=1, replica_groups=mesh['dp'=4,'row'=2,'col'=4] {'dp','row'}, use_global_device_ids=true, to_apply=%region_6.0 | all-reduce | flops 3584 | bytes 28672 | tf_op jit(solution)/shard_map/psum | solution.py:44
  350.3 1.5 multiply_reduce_fusion.3
  351.8 4.5 multiply_reduce_fusion.2
  356.3 37.1 %all-reduce = (f32[]{:T(128)}, f32[]{:T(128)}) all-reduce(f32[]{:T(128)} %multiply_reduce_fusion.2, f32[]{:T(128)} %multiply_reduce_fusion.3), channel_id=1, replica_groups=mesh['dp'=4,'row'=2,'col'=4] {'dp','row','col'}, use_global_device_ids=true, to_apply=%region_10.0 | all-reduce | flops 2 | bytes 16 | tf_op jit(solution)/shard_map/psum | solution.py:66
  394.1 3.9 multiply_subtract_fusion.1
  398.1 0.5 all-gather.13.cloned.1.call-update
  400.1 7.2 multiply_subtract_fusion
  407.3 0.5 all-gather.9.cloned.1.call-update
  407.9 79.4 %all-gather.11.cloned.1.call-done = f32[2048,1024]{1,0:T(8,128)} async-done(((f32[512,1024]{1,0:T(8,128)}), f32[2048,1024]{1,0:T(8,128)}) %all-gather.11.cloned.1.call-update) | async-done | bytes 8388624 | tf_op jit(solution)/shard_map/all_gather | solution.py:84
  487.3 89.9 %all-gather.13.cloned.1.call-done = f32[2048,1024]{1,0:T(8,128)} async-done(((f32[512,1024]{1,0:T(8,128)}), f32[2048,1024]{1,0:T(8,128)}) %all-gather.13.cloned.1.call-update) | async-done | bytes 8388624 | tf_op jit(solution)/shard_map/all_gather | solution.py:88
  577.2 195.5 %all-gather.7.cloned.1.call-done = f32[2048,2560]{1,0:T(8,128)} async-done(((f32[512,2560]{1,0:T(8,128)}), f32[2048,2560]{1,0:T(8,128)}) %all-gather.7.cloned.1.call-update) | async-done | bytes 20971536 | tf_op jit(solution)/shard_map/all_gather | solution.py:83
  772.7 195.5 %all-gather.9.cloned.1.call-done = f32[2048,2560]{1,0:T(8,128)} async-done(((f32[512,2560]{1,0:T(8,128)}), f32[2048,2560]{1,0:T(8,128)}) %all-gather.9.cloned.1.call-update) | async-done | bytes 20971536 | tf_op jit(solution)/shard_map/all_gather | solution.py:87
  968.2 18.0 %copy.22 = f32[2048,2560]{1,0:T(8,128)} copy(f32[2048,2560]{1,0:T(8,128)} %all-gather.7.cloned.1.call-done) | data formatting | bytes 41943040
  986.2 2.4 copy-done
  988.6 10.6 %copy.23 = f32[2048,2560]{1,0:T(8,128)} copy(f32[2048,2560]{1,0:T(8,128)S(1)} %copy-done) | data formatting | bytes 41943040
  999.3 3.6 copy.24
  1003.0 3.4 copy.25
  (41 shorter events, 0.5 us)
Async XLA Ops:
  7.2 93.0 %reduce-scatter.5.cloned.1.call-start = ((), (), s32[]{:S(2)}) async-start(), calls=%async_computation.5 | async-start | bytes 10485760 | tf_op jit(solution)/shard_map/reduce_scatter | solution.py:33
  7.9 283.5 %reduce-scatter.3.cloned.1.call-start = ((), (), s32[]{:S(2)}) async-start(), calls=%async_computation.2 | async-start | bytes 26214400 | tf_op jit(solution)/shard_map/reduce_scatter | solution.py:32
  8.7 478.6 %all-gather.11.cloned.1.call-start = ((), (), s32[]{:S(2)}) async-start(), calls=%async_computation.6 | async-start | bytes 10485760 | tf_op jit(solution)/shard_map/all_gather | solution.py:84
  8.7 10.1 %copy-start.3 = (bf16[2048,1024]{1,0:T(8,128)(2,1)S(1)}, bf16[2048,1024]{1,0:T(8,128)(2,1)}, u32[]{:S(2)}) copy-start(bf16[2048,1024]{1,0:T(8,128)(2,1)} %param.14) | copy-start | bytes 12582916
  18.8 302.9 %copy-start.9 = (f32[2048]{0:T(1024)S(1)}, f32[2048]{0:T(1024)}, u32[]{:S(2)}) copy-start(f32[2048]{0:T(1024)} %param.16) | copy-start | bytes 24580
  18.8 302.9 %copy-start.10 = (f32[2048]{0:T(1024)S(1)}, f32[2048]{0:T(1024)}, u32[]{:S(2)}) copy-start(f32[2048]{0:T(1024)} %param.12) | copy-start | bytes 24580
  18.8 331.4 %copy-start.11 = (f32[1024]{0:T(1024)S(1)}, f32[1024]{0:T(1024)}, u32[]{:S(2)}) copy-start(f32[1024]{0:T(1024)} %param.17) | copy-start | bytes 12292
  18.8 331.4 %copy-start.8 = (f32[2560]{0:T(1024)S(1)}, f32[2560]{0:T(1024)}, u32[]{:S(2)}) copy-start(f32[2560]{0:T(1024)} %param.13) | copy-start | bytes 30724
  100.2 250.1 %copy-start.1 = (f32[512,1024]{1,0:T(8,128)S(1)}, f32[512,1024]{1,0:T(8,128)}, u32[]{:S(2)}) copy-start(f32[512,1024]{1,0:T(8,128)} %reduce-scatter.5.cloned.1.call-done) | copy-start | bytes 6291460
  322.3 75.7 %copy-start.6 = (f32[2048]{0:T(1024)}, f32[2048]{0:T(1024)S(1)}, u32[]{:S(2)}) copy-start(f32[2048]{0:T(1024)S(1)} %get-tuple-element.46) | copy-start | bytes 24580
  322.3 75.7 %copy-start.7 = (f32[2048]{0:T(1024)}, f32[2048]{0:T(1024)S(1)}, u32[]{:S(2)}) copy-start(f32[2048]{0:T(1024)S(1)} %get-tuple-element.42) | copy-start | bytes 24580
  350.3 47.8 %copy-start.5 = (f32[1024]{0:T(1024)}, f32[1024]{0:T(1024)S(1)}, u32[]{:S(2)}) copy-start(f32[1024]{0:T(1024)S(1)} %multiply_add_fusion.5) | copy-start | bytes 12292
  350.3 49.7 %copy-start.4 = (f32[2560]{0:T(1024)}, f32[2560]{0:T(1024)S(1)}, u32[]{:S(2)}) copy-start(f32[2560]{0:T(1024)S(1)} %multiply_add_fusion.2) | copy-start | bytes 30724
  398.0 179.1 %all-gather.13.cloned.1.call-start = ((), (), s32[]{:S(2)}) async-start(), calls=%async_computation.7 | async-start | bytes 10485760 | tf_op jit(solution)/shard_map/all_gather | solution.py:88
  398.6 374.1 %all-gather.7.cloned.1.call-start = ((), (), s32[]{:S(2)}) async-start(), calls=%async_computation.3 | async-start | bytes 26214400 | tf_op jit(solution)/shard_map/all_gather | solution.py:83
  407.3 560.9 %all-gather.9.cloned.1.call-start = ((), (), s32[]{:S(2)}) async-start(), calls=%async_computation.4 | async-start | bytes 26214400 | tf_op jit(solution)/shard_map/all_gather | solution.py:87
  968.2 20.4 %copy-start = (f32[2048,2560]{1,0:T(8,128)S(1)}, f32[2048,2560]{1,0:T(8,128)}, u32[]{:S(2)}) copy-start(f32[2048,2560]{1,0:T(8,128)} %all-gather.9.cloned.1.call-done) | copy-start | bytes 62914564
  968.2 34.7 %slice-start = ((s8[8388608]{0:T(1024)(128)(4,1)}), s8[4194304]{0:T(1024)(128)(4,1)S(1)}, s32[]{:S(2)}) async-start(s8[8388608]{0:T(1024)(128)(4,1)} %bitcast.9), calls=%async_computation.8 | async-start | bytes 8388608
  988.6 10.6 %copy-start.2 = (f32[2048,1024]{1,0:T(8,128)S(1)}, f32[2048,1024]{1,0:T(8,128)}, u32[]{:S(2)}) copy-start(f32[2048,1024]{1,0:T(8,128)} %all-gather.11.cloned.1.call-done) | copy-start | bytes 25165828
  988.6 14.3 %slice-start.1 = ((s8[8388608]{0:T(1024)(128)(4,1)}), s8[4194304]{0:T(1024)(128)(4,1)S(1)}, s32[]{:S(2)}) async-start(s8[8388608]{0:T(1024)(128)(4,1)} %bitcast.9), calls=%async_computation.9 | async-start | bytes 8388608
Sparse Core Ops, SparseCore 0:
  11.1 89.0 reduce-scatter.4
  103.6 187.7 reduce-scatter.2
  398.2 89.0 all-gather.10
  489.5 87.5 all-gather.12
  579.5 193.1 all-gather.6
  775.0 193.1 all-gather.8
where the time goes:
time: 1010 us
  waiting for transfers between devices  810 us (80%)
  blocking collectives  110 us (11%)
  local copies, waits for them, and re-layouts  38.3 us (4%)
  other arithmetic  36.2 us (4%)
  between operations  19 us (2%)
    all_gather x1, waiting for transfers between devices, body(): lax.all_gather(clipped[0], 'dp', axis=0, tiled=True)  196 us
    all_gather x1, waiting for transfers between devices, body(): lax.all_gather(quarter_new[0], 'dp', axis=0, tiled=True)  196 us
    reduce_scatter x1, waiting for transfers between devices, body(): lax.psum_scatter(ffn_grads[0], 'dp', scatter_dimension=0, tiled=True)  189 us
    all_gather x1, waiting for transfers between devices, body(): lax.all_gather(clipped[1], 'dp', axis=0, tiled=True)  89.9 us
    all_gather x1, waiting for transfers between devices, body(): lax.all_gather(quarter_new[1], 'dp', axis=0, tiled=True)  79.4 us
    reduce_scatter x1, waiting for transfers between devices, body(): lax.psum_scatter(attn_grads[0], 'dp', scatter_dimension=0, tiled=True)  58.1 us
    unnamed x32, local copies, waits for them, and re-layouts  38.2 us
    psum x1, blocking collectives, body(): update_tot = lax.psum((update_sq[0], update_sq[1]), ('dp', 'row', 'col'))  37.1 us
  transfers between devices with their start and end apart: 6, of which 6 were waited for; matrix products, arithmetic and copies ran while one was open for 2% of the time, Pallas kernels for 0%

commit v1 on v0

--- a/solution.py
+++ b/solution.py
@@ -41,7 +41,8 @@
     row_sums = lax.psum(tuple((jnp.sum(s_part, axis=1) for s_part in squares)), "col")
     col_part = tuple((jnp.sum(s_part, axis=0) for s_part in squares))
     row_full = lax.all_gather(row_sums, "dp", axis=0, tiled=True)
-    col_sums = lax.psum(col_part, ("dp", "row"))
+    one_axis = lax.psum(col_part, "row")
+    col_sums = lax.psum(one_axis, "dp")
     rows_new = tuple(
         (
             decay * rows_old[index] + (1.0 - decay) * (row_full[index] / widths_out[index])

time: 1010 us -> 1010 us (level)
  no operation moved by 1% of the time
where the time goes in v1:
time: 1010 us
  waiting for transfers between devices  810 us (80%)
  blocking collectives  103 us (10%)
  local copies, waits for them, and re-layouts  38.3 us (4%)
  other arithmetic  36.2 us (4%)
  between operations  19 us (2%)
    all_gather x1, waiting for transfers between devices, body(): lax.all_gather(clipped[0], 'dp', axis=0, tiled=True)  196 us
    all_gather x1, waiting for transfers between devices, body(): lax.all_gather(quarter_new[0], 'dp', axis=0, tiled=True)  196 us
    reduce_scatter x1, waiting for transfers between devices, body(): lax.psum_scatter(ffn_grads[0], 'dp', scatter_dimension=0, tiled=True)  189 us
    all_gather x1, waiting for transfers between devices, body(): lax.all_gather(clipped[1], 'dp', axis=0, tiled=True)  89.9 us
    all_gather x1, waiting for transfers between devices, body(): lax.all_gather(quarter_new[1], 'dp', axis=0, tiled=True)  79.4 us
    reduce_scatter x1, waiting for transfers between devices, body(): lax.psum_scatter(attn_grads[0], 'dp', scatter_dimension=0, tiled=True)  58.1 us
    unnamed x32, local copies, waits for them, and re-layouts  38.2 us
    psum x1, blocking collectives, body(): update_tot = lax.psum((update_sq[0], update_sq[1]), ('dp', 'row', 'col'))  37.1 us
  transfers between devices with their start and end apart: 6, of which 6 were waited for; matrix products, arithmetic and copies ran while one was open for 2% of the time, Pallas kernels for 0%

profile of v1, /device:TPU:0, one launch (start us, length us, event | category | flops | bytes accessed | tf_op | source)
XLA Modules:
  0.0 1006.3 jit_solution(1410422167678306964)
XLA Ops:
  7.2 0.7 reduce-scatter.5.cloned.1.call-update
  7.9 0.7 reduce-scatter.3.cloned.1.call-update
  8.7 10.1 %multiply_reduce_fusion = f32[]{:T(128)} fusion(bf16[2048,2560]{1,0:T(8,128)(2,1)} %param.10), kind=kLoop, calls=%fused_computation | loop fusion | flops 15728639 | bytes 10485764 | tf_op jit(solution)/shard_map/reduce_sum | solution.py:69
  18.9 2.8 multiply_reduce_fusion.1
  21.6 19.1 %all-reduce.1 = (f32[]{:T(128)}, f32[]{:T(128)}) all-reduce(f32[]{:T(128)} %multiply_reduce_fusion, f32[]{:T(128)} %multiply_reduce_fusion.1), channel_id=1, replica_groups=mesh['dp'=4,'row'=2,'col'=4] {'row','col'}, use_global_device_ids=true, to_apply=%region_1.0 | all-reduce | flops 2 | bytes 16 | tf_op jit(solution)/shard_map/psum | solution.py:68
  42.2 58.1 %reduce-scatter.5.cloned.1.call-done = f32[512,1024]{1,0:T(8,128)} async-done(((f32[2048,1024]{1,0:T(8,128)}), f32[512,1024]{1,0:T(8,128)}) %reduce-scatter.5.cloned.1.call-update) | async-done | bytes 2097168 | tf_op jit(solution)/shard_map/reduce_scatter | solution.py:33
  100.2 2.1 fusion.2
  102.4 189.1 %reduce-scatter.3.cloned.1.call-done = f32[512,2560]{1,0:T(8,128)} async-done(((f32[2048,2560]{1,0:T(8,128)}), f32[512,2560]{1,0:T(8,128)}) %reduce-scatter.3.cloned.1.call-update) | async-done | bytes 5242896 | tf_op jit(solution)/shard_map/reduce_scatter | solution.py:32
  291.4 3.4 fusion
  294.9 11.7 %all-reduce.2 = (f32[512]{0:T(512)S(1)}, f32[512]{0:T(512)S(1)}) all-reduce(f32[512]{0:T(512)S(1)} %get-tuple-element.9, f32[512]{0:T(512)S(1)} %get-tuple-element.11), channel_id=1, replica_groups=mesh['dp'=4,'row'=2,'col'=4] {'col'}, use_global_device_ids=true, to_apply=%region_4.0 | all-reduce | flops 1024 | bytes 8192 | tf_op jit(solution)/shard_map/psum | solution.py:41
  306.5 7.9 all-gather.1
  314.5 7.2 all-gather
  321.7 0.6 fusion.4
  322.3 4.5 all-reduce.4
  328.1 0.1 dynamic_slice.15
  328.3 15.1 %all-reduce.3 = (f32[2560]{0:T(1024)S(1)}, f32[1024]{0:T(1024)S(1)}) all-reduce(f32[2560]{0:T(1024)S(1)} %get-tuple-element.21, f32[1024]{0:T(1024)S(1)} %get-tuple-element.22), channel_id=1, replica_groups=mesh['dp'=4,'row'=2,'col'=4] {'dp'}, use_global_device_ids=true, to_apply=%region_7.0 | all-reduce | flops 3584 | bytes 28672 | tf_op jit(solution)/shard_map/psum | solution.py:45
  343.4 1.5 multiply_reduce_fusion.3
  344.9 4.5 multiply_reduce_fusion.2
  349.4 37.1 %all-reduce = (f32[]{:T(128)}, f32[]{:T(128)}) all-reduce(f32[]{:T(128)} %multiply_reduce_fusion.2, f32[]{:T(128)} %multiply_reduce_fusion.3), channel_id=1, replica_groups=mesh['dp'=4,'row'=2,'col'=4] {'dp','row','col'}, use_global_device_ids=true, to_apply=%region_11.0 | all-reduce | flops 2 | bytes 16 | tf_op jit(solution)/shard_map/psum | solution.py:67
  387.2 3.9 multiply_subtract_fusion.1
  391.2 0.5 all-gather.13.cloned.1.call-update
  393.1 7.2 multiply_subtract_fusion
  400.4 0.5 all-gather.9.cloned.1.call-update
  401.0 79.4 %all-gather.11.cloned.1.call-done = f32[2048,1024]{1,0:T(8,128)} async-done(((f32[512,1024]{1,0:T(8,128)}), f32[2048,1024]{1,0:T(8,128)}) %all-gather.11.cloned.1.call-update) | async-done | bytes 8388624 | tf_op jit(solution)/shard_map/all_gather | solution.py:85
  480.3 89.9 %all-gather.13.cloned.1.call-done = f32[2048,1024]{1,0:T(8,128)} async-done(((f32[512,1024]{1,0:T(8,128)}), f32[2048,1024]{1,0:T(8,128)}) %all-gather.13.cloned.1.call-update) | async-done | bytes 8388624 | tf_op jit(solution)/shard_map/all_gather | solution.py:89
  570.3 195.5 %all-gather.7.cloned.1.call-done = f32[2048,2560]{1,0:T(8,128)} async-done(((f32[512,2560]{1,0:T(8,128)}), f32[2048,2560]{1,0:T(8,128)}) %all-gather.7.cloned.1.call-update) | async-done | bytes 20971536 | tf_op jit(solution)/shard_map/all_gather | solution.py:84
  765.8 195.5 %all-gather.9.cloned.1.call-done = f32[2048,2560]{1,0:T(8,128)} async-done(((f32[512,2560]{1,0:T(8,128)}), f32[2048,2560]{1,0:T(8,128)}) %all-gather.9.cloned.1.call-update) | async-done | bytes 20971536 | tf_op jit(solution)/shard_map/all_gather | solution.py:88
  961.3 18.0 %copy.22 = f32[2048,2560]{1,0:T(8,128)} copy(f32[2048,2560]{1,0:T(8,128)} %all-gather.7.cloned.1.call-done) | data formatting | bytes 41943040
  979.3 2.4 copy-done
  981.7 10.6 %copy.23 = f32[2048,2560]{1,0:T(8,128)} copy(f32[2048,2560]{1,0:T(8,128)S(1)} %copy-done) | data formatting | bytes 41943040
  992.3 3.6 copy.24
  996.1 3.4 copy.25
  (41 shorter events, 0.5 us)
Async XLA Ops:
  7.2 93.0 %reduce-scatter.5.cloned.1.call-start = ((), (), s32[]{:S(2)}) async-start(), calls=%async_computation.5 | async-start | bytes 10485760 | tf_op jit(solution)/shard_map/reduce_scatter | solution.py:33
  7.9 283.5 %reduce-scatter.3.cloned.1.call-start = ((), (), s32[]{:S(2)}) async-start(), calls=%async_computation.2 | async-start | bytes 26214400 | tf_op jit(solution)/shard_map/reduce_scatter | solution.py:32
  8.7 471.7 %all-gather.11.cloned.1.call-start = ((), (), s32[]{:S(2)}) async-start(), calls=%async_computation.6 | async-start | bytes 10485760 | tf_op jit(solution)/shard_map/all_gather | solution.py:85
  8.7 10.1 %copy-start.3 = (bf16[2048,1024]{1,0:T(8,128)(2,1)S(1)}, bf16[2048,1024]{1,0:T(8,128)(2,1)}, u32[]{:S(2)}) copy-start(bf16[2048,1024]{1,0:T(8,128)(2,1)} %param.14) | copy-start | bytes 12582916
  18.8 302.9 %copy-start.9 = (f32[2048]{0:T(1024)S(1)}, f32[2048]{0:T(1024)}, u32[]{:S(2)}) copy-start(f32[2048]{0:T(1024)} %param.16) | copy-start | bytes 24580
  18.8 302.9 %copy-start.10 = (f32[2048]{0:T(1024)S(1)}, f32[2048]{0:T(1024)}, u32[]{:S(2)}) copy-start(f32[2048]{0:T(1024)} %param.12) | copy-start | bytes 24580
  18.8 324.5 %copy-start.11 = (f32[1024]{0:T(1024)S(1)}, f32[1024]{0:T(1024)}, u32[]{:S(2)}) copy-start(f32[1024]{0:T(1024)} %param.17) | copy-start | bytes 12292
  18.8 324.5 %copy-start.8 = (f32[2560]{0:T(1024)S(1)}, f32[2560]{0:T(1024)}, u32[]{:S(2)}) copy-start(f32[2560]{0:T(1024)} %param.13) | copy-start | bytes 30724
  100.2 243.2 %copy-start.1 = (f32[512,1024]{1,0:T(8,128)S(1)}, f32[512,1024]{1,0:T(8,128)}, u32[]{:S(2)}) copy-start(f32[512,1024]{1,0:T(8,128)} %reduce-scatter.5.cloned.1.call-done) | copy-start | bytes 6291460
  322.3 68.8 %copy-start.6 = (f32[2048]{0:T(1024)}, f32[2048]{0:T(1024)S(1)}, u32[]{:S(2)}) copy-start(f32[2048]{0:T(1024)S(1)} %get-tuple-element.48) | copy-start | bytes 24580
  322.3 68.8 %copy-start.7 = (f32[2048]{0:T(1024)}, f32[2048]{0:T(1024)S(1)}, u32[]{:S(2)}) copy-start(f32[2048]{0:T(1024)S(1)} %get-tuple-element.44) | copy-start | bytes 24580
  343.3 47.8 %copy-start.5 = (f32[1024]{0:T(1024)}, f32[1024]{0:T(1024)S(1)}, u32[]{:S(2)}) copy-start(f32[1024]{0:T(1024)S(1)} %multiply_add_fusion.5) | copy-start | bytes 12292
  343.4 49.7 %copy-start.4 = (f32[2560]{0:T(1024)}, f32[2560]{0:T(1024)S(1)}, u32[]{:S(2)}) copy-start(f32[2560]{0:T(1024)S(1)} %multiply_add_fusion.2) | copy-start | bytes 30724
  391.1 179.1 %all-gather.13.cloned.1.call-start = ((), (), s32[]{:S(2)}) async-start(), calls=%async_computation.7 | async-start | bytes 10485760 | tf_op jit(solution)/shard_map/all_gather | solution.py:89
  391.7 374.1 %all-gather.7.cloned.1.call-start = ((), (), s32[]{:S(2)}) async-start(), calls=%async_computation.3 | async-start | bytes 26214400 | tf_op jit(solution)/shard_map/all_gather | solution.py:84
  400.4 560.9 %all-gather.9.cloned.1.call-start = ((), (), s32[]{:S(2)}) async-start(), calls=%async_computation.4 | async-start | bytes 26214400 | tf_op jit(solution)/shard_map/all_gather | solution.py:88
  961.3 20.4 %copy-start = (f32[2048,2560]{1,0:T(8,128)S(1)}, f32[2048,2560]{1,0:T(8,128)}, u32[]{:S(2)}) copy-start(f32[2048,2560]{1,0:T(8,128)} %all-gather.9.cloned.1.call-done) | copy-start | bytes 62914564
  961.3 34.7 %slice-start = ((s8[8388608]{0:T(1024)(128)(4,1)}), s8[4194304]{0:T(1024)(128)(4,1)S(1)}, s32[]{:S(2)}) async-start(s8[8388608]{0:T(1024)(128)(4,1)} %bitcast.9), calls=%async_computation.8 | async-start | bytes 8388608
  981.7 10.6 %copy-start.2 = (f32[2048,1024]{1,0:T(8,128)S(1)}, f32[2048,1024]{1,0:T(8,128)}, u32[]{:S(2)}) copy-start(f32[2048,1024]{1,0:T(8,128)} %all-gather.11.cloned.1.call-done) | copy-start | bytes 25165828
  981.7 14.3 %slice-start.1 = ((s8[8388608]{0:T(1024)(128)(4,1)}), s8[4194304]{0:T(1024)(128)(4,1)S(1)}, s32[]{:S(2)}) async-start(s8[8388608]{0:T(1024)(128)(4,1)} %bitcast.9), calls=%async_computation.9 | async-start | bytes 8388608
Sparse Core Ops, SparseCore 0:
  11.1 89.0 reduce-scatter.4
  103.6 187.7 reduce-scatter.2
  391.2 89.0 all-gather.10
  482.6 87.5 all-gather.12
  572.6 193.1 all-gather.6
  768.1 193.1 all-gather.8
